TPU v7x, 512 devices: a whole 4x4x16 slice. The times are simulated.
512 devices in a mesh: prow: 32 (over x, z_lo), pcol: 16 (over z_hi, y, core).
Axes of the slice: x: 4, y: 4, z: 16 (z_hi: 2, z_lo: 8; z = z_hi * 8 + z_lo), core: 2. Of those that a mesh axis runs over, the one named last changes fastest.
Arguments:
- inverse_part: float32 [12288, 12288], P('prow', 'pcol'), may hold values from -0.0546875 to 0.0546875
- lower_panel: float32 [12288, 2048], P('prow', 'pcol'), may hold values from -2 to 2
- struct_mask: int32 [16, 96], P('pcol', 'prow'), may hold values 0 or 1
- diag_inverse: float32 [16, 128, 128], P('pcol'), may hold values from -6 to 6
Outputs:
- off_diag: float32 [12288, 2048], P('prow', 'pcol')
- diag_block: float32 [16, 128, 128], P('pcol')
All inputs are finite; a program needn't handle non-finite values. No bound on the sum of `struct_mask` on one device may be relied on, other than what follows from the above.
Results may differ from a plain program's by a relative error of at most 0.00007.
Values sent between devices are 32-bit elements; how exact they have to be, the bound alone decides.
A program may use at most 64 MiB of HBM per device.

v0:
```python
import jax
import jax.numpy as jnp
from jax import lax
from jax.sharding import PartitionSpec as P


def from_root(array, axis, root):
    mine = lax.axis_index(axis) == root
    return lax.psum(jnp.where(mine, array, jnp.zeros_like(array)), axis)


def on_device(inverse_part, lower_panel, struct_mask, diag_inverse):
    col_count = lax.axis_size("pcol")
    row_count = lax.axis_size("prow")
    factor = row_count // col_count
    blocks = diag_inverse.shape[1]
    rows = lower_panel.shape[0]
    width = lower_panel.shape[1]
    row_blocks = rows // blocks
    sup_local = width // blocks
    member = jnp.transpose(struct_mask).astype(jnp.float32)
    masked = (
        lower_panel.reshape(row_blocks, blocks, sup_local, blocks) * member[:, None, :, None]
    ).reshape(rows, width)
    row_panel = lax.all_gather(masked, "pcol", axis=1, tiled=True)
    pieces = []
    for offset in range(factor):
        root = factor * lax.axis_index("pcol") + offset
        pieces.append(from_root(row_panel, "prow", root))
    needed = jnp.concatenate(pieces, axis=0)
    summed = lax.psum_scatter(
        lax.dot_general(
            needed,
            inverse_part,
            (((0,), (1,)), ((), ())),
            precision=lax.Precision.HIGHEST,
            preferred_element_type=jnp.float32,
        ),
        "pcol",
        scatter_dimension=0,
        tiled=True,
    )
    off_diag = -(
        jnp.transpose(summed).reshape(row_blocks, blocks, sup_local, blocks)
        * member[:, None, :, None]
    ).reshape(rows, width)
    local_corr = jnp.einsum(
        "ika,ikb->kab",
        masked.reshape(rows, sup_local, blocks),
        off_diag.reshape(rows, sup_local, blocks),
        precision=lax.Precision.HIGHEST,
    )
    total_corr = lax.psum(local_corr, "prow")
    diag_block = diag_inverse - total_corr
    return (off_diag, diag_block)


def solution(mesh):
    return jax.shard_map(
        on_device,
        mesh=mesh,
        in_specs=(P("prow", "pcol"), P("prow", "pcol"), P("pcol", "prow"), P("pcol", None, None)),
        out_specs=(P("prow", "pcol"), P("pcol", None, None)),
        check_vma=False,
    )
```

profile of v0, /device:TPU:1, one launch (start us, length us, event | category | flops | bytes accessed | tf_op | source)
XLA Modules:
  0.0 1184.0 jit_solution(7648962440932770573)
XLA Ops:
  7.2 0.0 copy-start
  7.2 0.0 all-gather.2.cloned.1.call-start
  7.2 0.7 convert_bitcast_fusion
  8.0 0.1 broadcast_bitcast_fusion
  8.0 1.7 broadcast_multiply_fusion
  9.8 0.0 all-gather.2.cloned.1.call-update
  9.8 0.0 all-reduce.6.cloned.1.call-start
  9.8 113.2 %all-gather.2.cloned.1.call-done = f32[384,2048]{1,0:T(8,128)} async-done(((f32[384,128]{1,0:T(8,128)}), f32[384,2048]{1,0:T(8,128)}) %all-gather.2.cloned.1.call-update) | async-done | bytes 3145744 | tf_op jit(solution)/shard_map/all_gather | solution.py:25
  123.0 5.5 broadcast_select_fusion.1
  128.5 0.0 all-reduce.6.cloned.1.call-update
  128.6 0.0 reduce-scatter.2.cloned.1.call-start
  128.6 473.8 %all-reduce.6.cloned.1.call-done = (f32[384,2048]{1,0:T(8,128)}, f32[384,2048]{1,0:T(8,128)}) async-done(((f32[384,2048]{1,0:T(8,128)}, f32[384,2048]{1,0:T(8,128)}), (f32[384,2048]{1,0:T(8,128)}, f32[384,2048]{1,0:T(8,128)})) %all-reduce.6.cloned.1.call-update) | async-done | bytes 6291472 | tf_op jit(solution)/shard_map/psum | solution.py:9
  602.4 0.0 copy-done
  602.4 22.9 %fusion = f32[2048,384]{1,0:T(8,128)} fusion(f32[384,768]{1,0:T(8,128)S(1)} %copy-done, f32[384,2048]{1,0:T(8,128)} %get-tuple-element.4, f32[384,2048]{1,0:T(8,128)} %get-tuple-element.5), kind=kOutput, calls=%fused_computation | convolution fusion | flops 7249330176 | bytes 10616832 | tf_op jit(solution)/shard_map/dot_general | solution.py:32
  625.3 0.0 copy-start.1
  625.3 0.0 copy-start.2
  625.3 0.0 reduce-scatter.2.cloned.1.call-update
  625.4 0.0 all-reduce.4.cloned.1.call-start
  625.4 153.0 %reduce-scatter.2.cloned.1.call-done = f32[128,384]{1,0:T(8,128)} async-done(((f32[2048,384]{1,0:T(8,128)}), f32[128,384]{1,0:T(8,128)}) %reduce-scatter.2.cloned.1.call-update) | async-done | bytes 196624 | tf_op jit(solution)/shard_map/reduce_scatter | solution.py:31
  778.5 0.0 copy-done.1
  778.5 2.1 convolution_bitcast_fusion
  780.6 0.0 all-reduce.4.cloned.1.call-update
  780.6 0.9 fusion.4
  781.6 0.8 copy.6
  782.4 393.6 %all-reduce.4.cloned.1.call-done = f32[1,128,128]{2,1,0:T(8,128)} async-done(((f32[1,128,128]{2,1,0:T(8,128)}), f32[1,128,128]{2,1,0:T(8,128)}) %all-reduce.4.cloned.1.call-update) | async-done | bytes 65552 | tf_op jit(solution)/shard_map/psum | solution.py:53
  1175.9 0.0 copy-done.2
  1175.9 1.5 sub.3
Async XLA Ops:
  7.2 595.2 %copy-start = (f32[384,768]{1,0:T(8,128)S(1)}, f32[384,768]{1,0:T(8,128)}, u32[]{:S(2)}) copy-start(f32[384,768]{1,0:T(8,128)} %param.4) | copy-start | bytes 3538948
  7.2 115.8 %all-gather.2.cloned.1.call-start = ((), (), s32[]{:S(2)}) async-start(), calls=%async_computation.1 | async-start | bytes 3342336 | tf_op jit(solution)/shard_map/all_gather | solution.py:25
  9.8 592.6 %all-reduce.6.cloned.1.call-start = ((), (), s32[]{:S(2)}) async-start(), calls=%async_computation.4 | async-start | bytes 12582912 | tf_op jit(solution)/shard_map/psum | solution.py:9
  128.6 649.9 %reduce-scatter.2.cloned.1.call-start = ((), (), s32[]{:S(2)}) async-start(), calls=%async_computation.2 | async-start | bytes 3342336 | tf_op jit(solution)/shard_map/reduce_scatter | solution.py:31
  625.3 153.1 %copy-start.1 = (f32[384,128]{1,0:T(8,128)S(1)}, f32[384,128]{1,0:T(8,128)}, u32[]{:S(2)}) copy-start(f32[384,128]{1,0:T(8,128)} %param.5) | copy-start | bytes 589828
  625.3 550.6 %copy-start.2 = (f32[1,128,128]{2,1,0:T(8,128)S(1)}, f32[1,128,128]{2,1,0:T(8,128)}, u32[]{:S(2)}) copy-start(f32[1,128,128]{2,1,0:T(8,128)} %param.7) | copy-start | bytes 196612
  625.4 550.6 %all-reduce.4.cloned.1.call-start = ((), (), s32[]{:S(2)}) async-start(), calls=%async_computation.3 | async-start | bytes 131072 | tf_op jit(solution)/shard_map/psum | solution.py:53
Sparse Core Ops, SparseCore 0:
  11.7 111.2 all-gather.1
  128.7 473.6 all-reduce.5
  625.5 152.9 reduce-scatter.1
  781.8 394.1 all-reduce.3
where the time goes:
time: 1190 us; the launch traced here: 1180 us
  waiting for transfers between devices  1130 us (95%)
  matrix products  25.1 us (2%)
  between operations  13.8 us (1%)
    psum x1, waiting for transfers between devices, from_root(): return lax.psum(jnp.where(mine, array, jnp.zeros_like(array)), axis)  474 us
    psum x1, waiting for transfers between devices, on_device(): total_corr = lax.psum(local_corr, 'prow')  394 us
    reduce_scatter x1, waiting for transfers between devices, on_device(): lax.psum_scatter(lax.dot_general(needed, inverse_part, (((0,), (1,)), (()...  153 us
    all_gather x1, waiting for transfers between devices, on_device(): row_panel = lax.all_gather(masked, 'pcol', axis=1, tiled=True)  113 us
  transfers between devices with their start and end apart: 4, of which 4 were waited for; matrix products, arithmetic and copies ran while one was open for 0% of the time, Pallas kernels for 0%

commit v1 on v0

v1 whole, which is shorter than its diff:
```python
import jax
import jax.numpy as jnp
from jax import lax
from jax.experimental import pallas as pl
from jax.experimental.pallas import tpu as pltpu
from jax.sharding import PartitionSpec as P

MESH = pl.DeviceIdType.MESH
X, ZL, ZH, Y = 4, 8, 2, 4
PIECES = 3
LAG = 4
LEAD = 2
TRAIL = 2


def split(value):
    high = value.astype(jnp.bfloat16)
    return high, (value - high.astype(jnp.float32)).astype(jnp.bfloat16)


def product(left_high, left_low, right):
    high, low = split(right)
    width = right.shape[1]
    both = jnp.dot(
        left_high, jnp.concatenate([high, low], axis=1), preferred_element_type=jnp.float32
    )
    rest = jnp.dot(left_low, high, preferred_element_type=jnp.float32)
    return both[:, :width] + (both[:, width:] + rest)


def copy_to(src, dst, send, recv, device):
    return pltpu.make_async_remote_copy(
        src_ref=src, dst_ref=dst, send_sem=send, recv_sem=recv,
        device_id=device, device_id_type=MESH,
    )


def kernel(
    a_hbm, l_hbm, mask_ref, dinv_hbm, off_ref, diag_ref,
    a_ref, l_ref, dinv_ref, masked, turned, a_in, a_high, a_low, m, p, c, yr, t, zb, cs, cx, cz, dg,
    fetch, s_a, r_a, s_first, s_right, s_left, s_x, r_m, s_c, r_c, s_y, r_y, s_z, r_z,
    s_cx, r_cx, s_cz, r_cz, s_dg, r_dg,
):
    row, col = lax.axis_index("prow"), lax.axis_index("pcol")
    x, zl = lax.div(row, ZL), lax.rem(row, ZL)
    zh, y, co = lax.div(col, 8), lax.rem(lax.div(col, 2), Y), lax.rem(col, 2)

    def device(x, zl, zh, y, co):
        return (x * ZL + zl, zh * 8 + y * 2 + co)

    kind = lax.rem(lax.div(x + 1, 2), 2)
    x_a, x_m = x + 1 - 2 * lax.rem(x, 2), 3 - x
    home = co == kind
    mine = lax.rem(lax.div(x, 2) + zh, 2)

    first_to = device(
        lax.rem(zl + lax.div(x, 2), 2) * 2 + lax.rem(lax.rem(zl + lax.div(x, 2), 2) + co, 2),
        2 * y + 1 - zh,
        lax.div(x, 2), 2 * lax.rem(x, 2) + lax.div(zl, 4), lax.rem(lax.div(zl, 2), 2),
    )
    first_slot = 2 * y + 1 - zh
    first_half = lax.rem(zl, 2)
    first_from = device(
        2 * zh + lax.div(y, 2),
        4 * lax.rem(y, 2) + 2 * co + mine,
        1 - lax.rem(zl, 2), lax.div(zl, 2), kind,
    )
    sibling = device(x, zl, zh, y, 1 - co)
    partner = device(x_m, zl, zh, y, co)
    a_partner = device(x_a, zl, zh, y, co)

    def x_peer(step):
        return device(lax.rem(x + step, X), zl, zh, y, co)

    def z_peer(step):
        return device(x, lax.rem(zl + step, ZL), zh, y, co)

    def y_peer(step):
        return device(x, zl, zh, lax.rem(y + step, Y), co)

    def end_peer(half):
        return device(jnp.where(home, x, x_a), zl, half, y, kind)

    fetch_l = pltpu.make_async_copy(l_hbm, l_ref, fetch.at[0])
    fetch_a = pltpu.make_async_copy(a_hbm, a_ref, fetch.at[1])
    fetch_dinv = pltpu.make_async_copy(dinv_hbm, dinv_ref, fetch.at[2])
    fetch_l.start()
    fetch_a.start()
    fetch_dinv.start()

    barrier = pltpu.get_barrier_semaphore()

    def greet(who):
        pl.semaphore_signal(barrier, inc=1, device_id=who, device_id_type=MESH)

    greet(first_from)
    greet(sibling)
    for step in range(1, X):
        greet(x_peer(step))
    for step in range(1, Y):
        greet(y_peer(step))
    for step in range(1, ZL):
        greet(z_peer(step))
    greet(end_peer(1 - zh))

    @pl.when(jnp.logical_not(home))
    def _():
        greet(end_peer(zh))

    fetch_l.wait()
    for block in range(3):
        rows = pl.ds(block * 128, 128)
        member = mask_ref[0, block].astype(jnp.float32)
        masked[rows, :] = l_ref[rows, :] * member

    pl.semaphore_wait(barrier, jnp.where(home, 16, 17))

    first = copy_to(
        masked, m.at[first_slot, first_half], s_first, r_m.at[first_slot, first_half], first_to
    )
    first.start()

    def send_a(piece):
        rows = pl.ds(piece * 128, 128)
        return copy_to(
            a_ref.at[rows, :], a_in.at[rows, :], s_a.at[piece], r_a.at[piece], a_partner
        )

    fetch_a.wait()
    high, low = split(a_ref[...])
    a_high[kind], a_low[kind] = high, low
    high, low = split(masked[...].T)
    turned[0], turned[1] = high, low

    def order(i):
        half = lax.div(i + 1, 2)
        near = jnp.where(lax.rem(i, 2) == 1, zl - half, zl + half)
        far = jnp.where(zl <= 3, i, 7 - i)
        return jnp.where(i <= 2 * jnp.minimum(zl, 7 - zl), near, far)

    def to_right(j):
        return copy_to(
            m.at[j, mine], m.at[j, mine], s_right.at[j], r_m.at[j, mine],
            device(x, jnp.minimum(zl + 1, 7), zh, y, co),
        )

    def to_left(j):
        return copy_to(
            m.at[j, mine], m.at[j, mine], s_left.at[j], r_m.at[j, mine],
            device(x, jnp.maximum(zl - 1, 0), zh, y, co),
        )

    def to_partner(j):
        return copy_to(m.at[j, mine], m.at[j, mine], s_x.at[j], r_m.at[j, mine], partner)

    def arrival(j, half):
        return copy_to(m.at[j, half], m.at[j, half], s_first, r_m.at[j, half], partner)

    def to_sibling(j):
        return copy_to(p.at[j, 1 - co], c.at[j], s_c.at[j], r_c.at[j], sibling)

    def to_owner(j):
        owner = lax.div(j, 2)
        slot = lax.rem(y - owner + Y, Y) - 1
        half = 1 - lax.rem(j, 2)
        return copy_to(
            p.at[j, co], yr.at[half, slot], s_y.at[j], r_y.at[half, slot],
            device(x, zl, zh, owner, co),
        )

    def to_end(half):
        return copy_to(t.at[half], zb.at[zh], s_z.at[half], r_z.at[zh], end_peer(half))

    def goes_right(j):
        return jnp.logical_and(j <= zl, zl < 7)

    def goes_left(j):
        return jnp.logical_and(j >= zl, zl > 0)

    def part(j, q):
        p[j, q] = product(a_high[q], a_low[q], m[j].reshape(768, 128))

    def step(i, carry):
        @pl.when(i < 8)
        def _():
            j = order(i)
            arrival(j, mine).wait_recv()
            to_partner(j).start()

            @pl.when(goes_right(j))
            def _():
                to_right(j).start()

            @pl.when(goes_left(j))
            def _():
                to_left(j).start()

        for piece in range(PIECES):

            @pl.when(i == piece)
            def _(piece=piece):
                send_a(piece).start()

        @pl.when(jnp.logical_and(i >= LEAD, i < LEAD + 8))
        def _():
            j = order(i - LEAD)
            arrival(j, 1 - mine).wait_recv()
            part(j, kind)

            @pl.when(jnp.logical_not(home))
            def _():
                to_sibling(j).start()

        @pl.when(i == LAG)
        def _():
            for piece in range(PIECES):
                send_a(piece).wait_recv()
            high, low = split(a_in[...])
            a_high[1 - kind], a_low[1 - kind] = high, low

        @pl.when(jnp.logical_and(i >= LAG, i < LAG + 8))
        def _():
            j = order(i - LAG)
            part(j, 1 - kind)

            @pl.when(home)
            def _():
                to_sibling(j).start()

        k = i - jnp.where(home, LEAD + 1, LAG + 1)

        @pl.when(jnp.logical_and(k >= 0, k < 8))
        def _():
            j = order(k)
            to_sibling(j).wait_recv()
            p[j, co] = p[j, co] + c[j]

            @pl.when(lax.div(j, 2) != y)
            def _():
                to_owner(j).start()

        @pl.when(jnp.logical_and(k >= TRAIL, k < TRAIL + 8))
        def _():
            j = order(k - TRAIL)
            half = 1 - lax.rem(j, 2)

            @pl.when(lax.div(j, 2) == y)
            def _():
                for slot in range(3):
                    copy_to(
                        t.at[0], yr.at[half, slot], s_y.at[0], r_y.at[half, slot], sibling
                    ).wait_recv()
                total = (p[j, co] + yr[half, 0]) + (yr[half, 1] + yr[half, 2])
                stays = jnp.logical_and(home, half == zh)

                @pl.when(stays)
                def _():
                    zb[zh] = total

                @pl.when(jnp.logical_not(stays))
                def _():
                    t[half] = total
                    to_end(half).start()

        return carry

    lax.fori_loop(0, 8 + LAG + 1 + TRAIL, step, 0)

    def end_arrival(half):
        return copy_to(t.at[0], zb.at[half], s_z.at[0], r_z.at[half], sibling)

    end_arrival(1 - zh).wait_recv()

    @pl.when(jnp.logical_not(home))
    def _():
        end_arrival(zh).wait_recv()

    for block in range(3):
        rows = pl.ds(block * 128, 128)
        member = mask_ref[0, block].astype(jnp.float32)
        off_ref[rows, :] = -((zb[0, rows, :] + zb[1, rows, :]) * member)

    correction = product(turned[0], turned[1], off_ref[...])
    for other in range(X):
        cs[other] = correction[other * 32 : other * 32 + 32, :]

    def corr_x(step):
        return copy_to(
            cs.at[lax.rem(x + step, X)], cx.at[step - 1], s_cx.at[step - 1], r_cx.at[step - 1],
            x_peer(step),
        )

    def corr_z(step):
        return copy_to(cz.at[zl], cz.at[zl], s_cz.at[step - 1], r_cz.at[zl], z_peer(step))

    def corr_back(step):
        return copy_to(dg.at[x], dg.at[x], s_dg.at[step - 1], r_dg.at[x], x_peer(step))

    for step_ in range(1, X):
        corr_x(step_).start()
    for step_ in range(1, X):
        corr_x(step_).wait_recv()
    cz[zl] = (cs[x] + cx[0]) + (cx[1] + cx[2])
    for step_ in range(1, ZL):
        corr_z(step_).start()
    for step_ in range(1, ZL):
        other = lax.rem(zl + step_, ZL)
        copy_to(cz.at[other], cz.at[other], s_cz.at[0], r_cz.at[other], sibling).wait_recv()
    dg[x] = ((cz[0] + cz[1]) + (cz[2] + cz[3])) + ((cz[4] + cz[5]) + (cz[6] + cz[7]))
    for step_ in range(1, X):
        corr_back(step_).start()
    for step_ in range(1, X):
        other = lax.rem(x + step_, X)
        copy_to(dg.at[other], dg.at[other], s_dg.at[0], r_dg.at[other], sibling).wait_recv()
    fetch_dinv.wait()
    for other in range(X):
        rows = pl.ds(other * 32, 32)
        diag_ref[0, rows, :] = dinv_ref[0, rows, :] - dg[other]

    first.wait_send()
    for piece in range(PIECES):
        send_a(piece).wait_send()

    def finish(j, carry):
        to_partner(j).wait_send()
        to_sibling(j).wait_send()

        @pl.when(goes_right(j))
        def _():
            to_right(j).wait_send()

        @pl.when(goes_left(j))
        def _():
            to_left(j).wait_send()

        @pl.when(lax.div(j, 2) != y)
        def _():
            to_owner(j).wait_send()

        return carry

    lax.fori_loop(0, 8, finish, 0)
    to_end(1 - zh).wait_send()

    @pl.when(jnp.logical_not(home))
    def _():
        to_end(zh).wait_send()

    for step_ in range(1, X):
        corr_x(step_).wait_send()
        corr_back(step_).wait_send()
    for step_ in range(1, ZL):
        corr_z(step_).wait_send()


def on_device(inverse_part, lower_panel, struct_mask, diag_inverse):
    f32, bf16 = jnp.float32, jnp.bfloat16
    dma = pltpu.SemaphoreType.DMA
    hbm = pl.BlockSpec(memory_space=pl.ANY)
    vmem = pl.BlockSpec(memory_space=pltpu.VMEM)
    return tuple(
        pl.pallas_call(
            kernel,
            out_shape=(
                jax.ShapeDtypeStruct((384, 128), f32),
                jax.ShapeDtypeStruct((1, 128, 128), f32),
            ),
            in_specs=[hbm, hbm, pl.BlockSpec(memory_space=pltpu.SMEM), hbm],
            out_specs=(vmem, vmem),
            scratch_shapes=[
                pltpu.VMEM((384, 768), f32),
                pltpu.VMEM((384, 128), f32),
                pltpu.VMEM((1, 128, 128), f32),
                pltpu.VMEM((384, 128), f32),
                pltpu.VMEM((2, 128, 384), bf16),
                pltpu.VMEM((384, 768), f32),
                pltpu.VMEM((2, 384, 768), bf16),
                pltpu.VMEM((2, 384, 768), bf16),
                pltpu.VMEM((8, 2, 384, 128), f32),
                pltpu.VMEM((8, 2, 384, 128), f32),
                pltpu.VMEM((8, 384, 128), f32),
                pltpu.VMEM((2, 3, 384, 128), f32),
                pltpu.VMEM((2, 384, 128), f32),
                pltpu.VMEM((2, 384, 128), f32),
                pltpu.VMEM((4, 32, 128), f32),
                pltpu.VMEM((3, 32, 128), f32),
                pltpu.VMEM((8, 32, 128), f32),
                pltpu.VMEM((4, 32, 128), f32),
                dma((3,)), dma((PIECES,)), dma((PIECES,)), dma,
                dma((8,)), dma((8,)), dma((8,)), dma((8, 2)),
                dma((8,)), dma((8,)), dma((8,)), dma((2, 3)), dma((2,)), dma((2,)),
                dma((3,)), dma((3,)), dma((7,)), dma((8,)), dma((3,)), dma((4,)),
            ],
            compiler_params=pltpu.CompilerParams(
                collective_id=0, has_side_effects=True, vmem_limit_bytes=48 * 1024 * 1024
            ),
            cost_estimate=pl.CostEstimate(
                flops=2 * 3 * 384 * 768 * 2048, bytes_accessed=4_000_000, transcendentals=0
            ),
        )(inverse_part, lower_panel, struct_mask, diag_inverse)
    )


def solution(mesh):
    return jax.shard_map(
        on_device,
        mesh=mesh,
        in_specs=(P("prow", "pcol"), P("prow", "pcol"), P("pcol", "prow"), P("pcol", None, None)),
        out_specs=(P("prow", "pcol"), P("pcol", None, None)),
        check_vma=False,
    )
```

time: 1190 us -> 153 us (0.13)
  the two profiles are of different devices: /device:TPU:1 before, /device:TPU:56 now
where the time goes in v1:
time: 153 us
  Pallas kernels  147 us (96%)
  local copies, waits for them, and re-layouts  4.99 us (3%)
    pallas_call x1, Pallas kernels, on_device(): pl.pallas_call(kernel, out_shape=(jax.ShapeDtypeStruct((384, 128), f32),...  147 us
    unnamed x10, local copies, waits for them, and re-layouts  4.99 us

profile of v1, /device:TPU:56, one launch (start us, length us, event | category | flops | bytes accessed | tf_op | source)
XLA Modules:
  0.0 152.9 jit_solution(12779285451025797523)
XLA Ops:
  0.6 0.0 copy-start
  0.6 1.3 copy-done
  1.9 0.0 copy-start.1
  1.9 0.9 copy-done.1
  2.8 0.0 copy-start.2
  2.8 0.8 copy-done.2
  3.7 0.0 copy-start.3
  3.7 0.7 copy-done.3
  4.3 147.3 %shard_map.59 = (f32[384,128]{1,0:T(8,128)S(1)}, f32[1,128,128]{2,1,0:T(8,128)S(1)}) custom-call(f32[384,768]{1,0:T(8,128)S(1)} %copy-done, f32[384,128]{1,0:T(8,128)S(1)} %copy-done.1, s32[1,3]{1,0:T(1,128)S(1)} %copy-done.3, f32[1,128,128]{2,1,0:T(8,128)S(1)} %copy-done.2), custom_call_target="tpu_custom_call" | custom-call | flops 3623878656 | bytes 4000000 | tf_op jit(solution)/shard_map/pallas_call | solution.py:362
  151.6 0.7 copy.8
  152.3 0.6 copy.9
Async XLA Ops:
  0.6 1.3 copy-start
  1.9 0.9 copy-start.1
  2.8 0.8 copy-start.2
  3.7 0.7 copy-start.3

commit v2 on v1

--- a/solution.py
+++ b/solution.py
@@ -8,9 +8,10 @@
 MESH = pl.DeviceIdType.MESH
 X, ZL, ZH, Y = 4, 8, 2, 4
 PIECES = 3
-LAG = 4
+PARTS = 2
+LAG = 6
 LEAD = 2
-TRAIL = 2
+TRAIL = 3
 
 
 def split(value):
@@ -115,10 +116,18 @@
 
     pl.semaphore_wait(barrier, jnp.where(home, 16, 17))
 
-    first = copy_to(
-        masked, m.at[first_slot, first_half], s_first, r_m.at[first_slot, first_half], first_to
-    )
-    first.start()
+    def spot(j, half, part):
+        return m.at[j, half, pl.ds(part * (384 // PARTS), 384 // PARTS), :]
+
+    def first(part):
+        return copy_to(
+            masked.at[pl.ds(part * (384 // PARTS), 384 // PARTS), :],
+            spot(first_slot, first_half, part),
+            s_first.at[part], r_m.at[first_slot, first_half, part], first_to,
+        )
+
+    for part in range(PARTS):
+        first(part).start()
 
     def send_a(piece):
         rows = pl.ds(piece * 128, 128)
@@ -127,6 +136,8 @@
         )
 
     fetch_a.wait()
+    for piece in range(PIECES):
+        send_a(piece).start()
     high, low = split(a_ref[...])
     a_high[kind], a_low[kind] = high, low
     high, low = split(masked[...].T)
@@ -138,23 +149,27 @@
         far = jnp.where(zl <= 3, i, 7 - i)
         return jnp.where(i <= 2 * jnp.minimum(zl, 7 - zl), near, far)
 
-    def to_right(j):
-        return copy_to(
-            m.at[j, mine], m.at[j, mine], s_right.at[j], r_m.at[j, mine],
+    def to_right(j, part):
+        here = spot(j, mine, part)
+        return copy_to(
+            here, here, s_right.at[j, part], r_m.at[j, mine, part],
             device(x, jnp.minimum(zl + 1, 7), zh, y, co),
         )
 
-    def to_left(j):
-        return copy_to(
-            m.at[j, mine], m.at[j, mine], s_left.at[j], r_m.at[j, mine],
+    def to_left(j, part):
+        here = spot(j, mine, part)
+        return copy_to(
+            here, here, s_left.at[j, part], r_m.at[j, mine, part],
             device(x, jnp.maximum(zl - 1, 0), zh, y, co),
         )
 
-    def to_partner(j):
-        return copy_to(m.at[j, mine], m.at[j, mine], s_x.at[j], r_m.at[j, mine], partner)
-
-    def arrival(j, half):
-        return copy_to(m.at[j, half], m.at[j, half], s_first, r_m.at[j, half], partner)
+    def to_partner(j, part):
+        here = spot(j, mine, part)
+        return copy_to(here, here, s_x.at[j, part], r_m.at[j, mine, part], partner)
+
+    def arrival(j, half, part):
+        here = spot(j, half, part)
+        return copy_to(here, here, s_first.at[0], r_m.at[j, half, part], partner)
 
     def to_sibling(j):
         return copy_to(p.at[j, 1 - co], c.at[j], s_c.at[j], r_c.at[j], sibling)
@@ -177,35 +192,33 @@
     def goes_left(j):
         return jnp.logical_and(j >= zl, zl > 0)
 
-    def part(j, q):
+    def multiply(j, q):
         p[j, q] = product(a_high[q], a_low[q], m[j].reshape(768, 128))
 
     def step(i, carry):
         @pl.when(i < 8)
         def _():
             j = order(i)
-            arrival(j, mine).wait_recv()
-            to_partner(j).start()
-
-            @pl.when(goes_right(j))
-            def _():
-                to_right(j).start()
-
-            @pl.when(goes_left(j))
-            def _():
-                to_left(j).start()
-
-        for piece in range(PIECES):
-
-            @pl.when(i == piece)
-            def _(piece=piece):
-                send_a(piece).start()
+            right, left = goes_right(j), goes_left(j)
+            for part in range(PARTS):
+                arrival(j, mine, part).wait_recv()
+
+                @pl.when(right)
+                def _(part=part):
+                    to_right(j, part).start()
+
+                @pl.when(left)
+                def _(part=part):
+                    to_left(j, part).start()
+
+                to_partner(j, part).start()
 
         @pl.when(jnp.logical_and(i >= LEAD, i < LEAD + 8))
         def _():
             j = order(i - LEAD)
-            arrival(j, 1 - mine).wait_recv()
-            part(j, kind)
+            for part in range(PARTS):
+                arrival(j, 1 - mine, part).wait_recv()
+            multiply(j, kind)
 
             @pl.when(jnp.logical_not(home))
             def _():
@@ -221,7 +234,7 @@
         @pl.when(jnp.logical_and(i >= LAG, i < LAG + 8))
         def _():
             j = order(i - LAG)
-            part(j, 1 - kind)
+            multiply(j, 1 - kind)
 
             @pl.when(home)
             def _():
@@ -317,21 +330,23 @@
         rows = pl.ds(other * 32, 32)
         diag_ref[0, rows, :] = dinv_ref[0, rows, :] - dg[other]
 
-    first.wait_send()
+    for part in range(PARTS):
+        first(part).wait_send()
     for piece in range(PIECES):
         send_a(piece).wait_send()
 
     def finish(j, carry):
-        to_partner(j).wait_send()
         to_sibling(j).wait_send()
-
-        @pl.when(goes_right(j))
-        def _():
-            to_right(j).wait_send()
-
-        @pl.when(goes_left(j))
-        def _():
-            to_left(j).wait_send()
+        for part in range(PARTS):
+            to_partner(j, part).wait_send()
+
+            @pl.when(goes_right(j))
+            def _(part=part):
+                to_right(j, part).wait_send()
+
+            @pl.when(goes_left(j))
+            def _(part=part):
+                to_left(j, part).wait_send()
 
         @pl.when(lax.div(j, 2) != y)
         def _():
@@ -386,13 +401,13 @@
                 pltpu.VMEM((3, 32, 128), f32),
                 pltpu.VMEM((8, 32, 128), f32),
                 pltpu.VMEM((4, 32, 128), f32),
-                dma((3,)), dma((PIECES,)), dma((PIECES,)), dma,
-                dma((8,)), dma((8,)), dma((8,)), dma((8, 2)),
+                dma((3,)), dma((PIECES,)), dma((PIECES,)), dma((PARTS,)),
+                dma((8, PARTS)), dma((8, PARTS)), dma((8, PARTS)), dma((8, 2, PARTS)),
                 dma((8,)), dma((8,)), dma((8,)), dma((2, 3)), dma((2,)), dma((2,)),
                 dma((3,)), dma((3,)), dma((7,)), dma((8,)), dma((3,)), dma((4,)),
             ],
             compiler_params=pltpu.CompilerParams(
-                collective_id=0, has_side_effects=True, vmem_limit_bytes=48 * 1024 * 1024
+                collective_id=0, has_side_effects=True, vmem_limit_bytes=63 * 1024 * 1024
             ),
             cost_estimate=pl.CostEstimate(
                 flops=2 * 3 * 384 * 768 * 2048, bytes_accessed=4_000_000, transcendentals=0

time: 153 us -> 140 us (0.915)
  the two profiles are of different devices: /device:TPU:56 before, /device:TPU:2 now
where the time goes in v2:
time: 140 us
  Pallas kernels  136 us (97%)
  local copies, waits for them, and re-layouts  3.09 us (2%)
    pallas_call x1, Pallas kernels, on_device(): pl.pallas_call(kernel, out_shape=(jax.ShapeDtypeStruct((384, 128), f32),...  136 us
    unnamed x2, local copies, waits for them, and re-layouts  3.09 us

profile of v2, /device:TPU:2, one launch (start us, length us, event | category | flops | bytes accessed | tf_op | source)
XLA Modules:
  0.0 140.0 jit_solution(15694697977194443624)
XLA Ops:
  0.6 136.3 %shard_map.59 = (f32[384,128]{1,0:T(8,128)}, f32[1,128,128]{2,1,0:T(8,128)}) custom-call(f32[384,768]{1,0:T(8,128)} %a_hbm.1, f32[384,128]{1,0:T(8,128)} %l_hbm.1, s32[1,3]{1,0:T(1,128)} %mask_ref.1, f32[1,128,128]{2,1,0:T(8,128)} %dinv_hbm.1), custom_call_target="tpu_custom_call" | custom-call | flops 3623878656 | bytes 4000000 | tf_op jit(solution)/shard_map/pallas_call | solution.py:377
  136.9 1.6 %copy.8 = f32[384,128]{1,0:T(8,128)} copy(f32[384,128]{1,0:T(8,128)} %get-tuple-element.4) | data formatting | bytes 393216
  138.5 1.5 %copy.9 = f32[1,128,128]{2,1,0:T(8,128)} copy(f32[1,128,128]{2,1,0:T(8,128)} %get-tuple-element.5) | data formatting | bytes 131072

commit v3 on v2

--- a/solution.py
+++ b/solution.py
@@ -8,10 +8,11 @@
 MESH = pl.DeviceIdType.MESH
 X, ZL, ZH, Y = 4, 8, 2, 4
 PIECES = 3
-PARTS = 2
-LAG = 6
+PARTS = 3
+LAG = 4
 LEAD = 2
-TRAIL = 3
+PASS = 2
+TRAIL = 4
 
 
 def split(value):
@@ -38,8 +39,8 @@
 
 def kernel(
     a_hbm, l_hbm, mask_ref, dinv_hbm, off_ref, diag_ref,
-    a_ref, l_ref, dinv_ref, masked, turned, a_in, a_high, a_low, m, p, c, yr, t, zb, cs, cx, cz, dg,
-    fetch, s_a, r_a, s_first, s_right, s_left, s_x, r_m, s_c, r_c, s_y, r_y, s_z, r_z,
+    a_ref, l_ref, dinv_ref, masked, turned, a_in, a_high, a_low, m, p, c, far, yr, t, zb, cs, cx, cz, dg,
+    fetch, s_a, r_a, s_first, s_right, s_left, s_x, r_m, s_c, r_c, s_y, r_y, r_far, s_z, r_z,
     s_cx, r_cx, s_cz, r_cz, s_dg, r_dg,
 ):
     row, col = lax.axis_index("prow"), lax.axis_index("pcol")
@@ -174,13 +175,25 @@
     def to_sibling(j):
         return copy_to(p.at[j, 1 - co], c.at[j], s_c.at[j], r_c.at[j], sibling)
 
+    def role(j):
+        half = 1 - lax.rem(j, 2)
+        toward = 1 - 2 * half
+        return lax.rem(y - lax.div(j, 2) + Y, Y), half, toward
+
     def to_owner(j):
+        _, half, toward = role(j)
         owner = lax.div(j, 2)
-        slot = lax.rem(y - owner + Y, Y) - 1
-        half = 1 - lax.rem(j, 2)
-        return copy_to(
-            p.at[j, co], yr.at[half, slot], s_y.at[j], r_y.at[half, slot],
+        side = jnp.where(lax.rem(y - owner + Y, Y) == 1, 0, 1)
+        return copy_to(
+            p.at[j, co], yr.at[half, side], s_y.at[j], r_y.at[half, side],
             device(x, zl, zh, owner, co),
+        )
+
+    def to_between(j):
+        _, half, toward = role(j)
+        return copy_to(
+            p.at[j, co], far.at[half], s_y.at[j], r_far.at[half],
+            device(x, zl, zh, lax.rem(y - toward + Y, Y), co),
         )
 
     def to_end(half):
@@ -248,8 +261,25 @@
             to_sibling(j).wait_recv()
             p[j, co] = p[j, co] + c[j]
 
-            @pl.when(lax.div(j, 2) != y)
-            def _():
+            distance, _, toward = role(j)
+
+            @pl.when(distance == lax.rem(Y - toward, Y))
+            def _():
+                to_owner(j).start()
+
+            @pl.when(distance == 2)
+            def _():
+                to_between(j).start()
+
+        @pl.when(jnp.logical_and(k >= PASS, k < PASS + 8))
+        def _():
+            j = order(k - PASS)
+            distance, half, toward = role(j)
+
+            @pl.when(distance == lax.rem(Y + toward, Y))
+            def _():
+                copy_to(t.at[0], far.at[half], s_y.at[0], r_far.at[half], sibling).wait_recv()
+                p[j, co] = p[j, co] + far[half]
                 to_owner(j).start()
 
         @pl.when(jnp.logical_and(k >= TRAIL, k < TRAIL + 8))
@@ -259,11 +289,11 @@
 
             @pl.when(lax.div(j, 2) == y)
             def _():
-                for slot in range(3):
+                for slot in range(2):
                     copy_to(
                         t.at[0], yr.at[half, slot], s_y.at[0], r_y.at[half, slot], sibling
                     ).wait_recv()
-                total = (p[j, co] + yr[half, 0]) + (yr[half, 1] + yr[half, 2])
+                total = p[j, co] + (yr[half, 0] + yr[half, 1])
                 stays = jnp.logical_and(home, half == zh)
 
                 @pl.when(stays)
@@ -348,7 +378,13 @@
             def _(part=part):
                 to_left(j, part).wait_send()
 
-        @pl.when(lax.div(j, 2) != y)
+        distance, _, _ = role(j)
+
+        @pl.when(distance == 2)
+        def _():
+            to_between(j).wait_send()
+
+        @pl.when(lax.rem(distance, 2) == 1)
         def _():
             to_owner(j).wait_send()
 
@@ -394,7 +430,8 @@
                 pltpu.VMEM((8, 2, 384, 128), f32),
                 pltpu.VMEM((8, 2, 384, 128), f32),
                 pltpu.VMEM((8, 384, 128), f32),
-                pltpu.VMEM((2, 3, 384, 128), f32),
+                pltpu.VMEM((2, 384, 128), f32),
+                pltpu.VMEM((2, 2, 384, 128), f32),
                 pltpu.VMEM((2, 384, 128), f32),
                 pltpu.VMEM((2, 384, 128), f32),
                 pltpu.VMEM((4, 32, 128), f32),
@@ -403,7 +440,7 @@
                 pltpu.VMEM((4, 32, 128), f32),
                 dma((3,)), dma((PIECES,)), dma((PIECES,)), dma((PARTS,)),
                 dma((8, PARTS)), dma((8, PARTS)), dma((8, PARTS)), dma((8, 2, PARTS)),
-                dma((8,)), dma((8,)), dma((8,)), dma((2, 3)), dma((2,)), dma((2,)),
+                dma((8,)), dma((8,)), dma((8,)), dma((2, 2)), dma((2,)), dma((2,)), dma((2,)),
                 dma((3,)), dma((3,)), dma((7,)), dma((8,)), dma((3,)), dma((4,)),
             ],
             compiler_params=pltpu.CompilerParams(

time: 140 us -> 138 us (0.986)
  Pallas kernels: 136 us -> 134 us
    pallas_call x1, Pallas kernels: 136 us -> 134 us  [on_device(): pl.pallas_call(kernel, out_shape=(jax.ShapeDtypeStruct((384, 128), f32),...]
where the time goes in v3:
time: 138 us
  Pallas kernels  134 us (97%)
  local copies, waits for them, and re-layouts  3.09 us (2%)
    pallas_call x1, Pallas kernels, on_device(): pl.pallas_call(kernel, out_shape=(jax.ShapeDtypeStruct((384, 128), f32),...  134 us
    unnamed x2, local copies, waits for them, and re-layouts  3.09 us

profile of v3, /device:TPU:2, one launch (start us, length us, event | category | flops | bytes accessed | tf_op | source)
XLA Modules:
  0.0 137.7 jit_solution(7403936425292588470)
XLA Ops:
  0.6 134.0 %shard_map.59 = (f32[384,128]{1,0:T(8,128)}, f32[1,128,128]{2,1,0:T(8,128)}) custom-call(f32[384,768]{1,0:T(8,128)} %a_hbm.1, f32[384,128]{1,0:T(8,128)} %l_hbm.1, s32[1,3]{1,0:T(1,128)} %mask_ref.1, f32[1,128,128]{2,1,0:T(8,128)} %dinv_hbm.1), custom_call_target="tpu_custom_call" | custom-call | flops 3623878656 | bytes 4000000 | tf_op jit(solution)/shard_map/pallas_call | solution.py:413
  134.6 1.6 %copy.8 = f32[384,128]{1,0:T(8,128)} copy(f32[384,128]{1,0:T(8,128)} %get-tuple-element.4) | data formatting | bytes 393216
  136.2 1.5 %copy.9 = f32[1,128,128]{2,1,0:T(8,128)} copy(f32[1,128,128]{2,1,0:T(8,128)} %get-tuple-element.5) | data formatting | bytes 131072

commit v4 on v3

--- a/solution.py
+++ b/solution.py
@@ -9,8 +9,7 @@
 X, ZL, ZH, Y = 4, 8, 2, 4
 PIECES = 3
 PARTS = 3
-LAG = 4
-LEAD = 2
+LAG = 3
 PASS = 2
 TRAIL = 4
 
@@ -205,9 +204,6 @@
     def goes_left(j):
         return jnp.logical_and(j >= zl, zl > 0)
 
-    def multiply(j, q):
-        p[j, q] = product(a_high[q], a_low[q], m[j].reshape(768, 128))
-
     def step(i, carry):
         @pl.when(i < 8)
         def _():
@@ -226,17 +222,6 @@
 
                 to_partner(j, part).start()
 
-        @pl.when(jnp.logical_and(i >= LEAD, i < LEAD + 8))
-        def _():
-            j = order(i - LEAD)
-            for part in range(PARTS):
-                arrival(j, 1 - mine, part).wait_recv()
-            multiply(j, kind)
-
-            @pl.when(jnp.logical_not(home))
-            def _():
-                to_sibling(j).start()
-
         @pl.when(i == LAG)
         def _():
             for piece in range(PIECES):
@@ -247,13 +232,14 @@
         @pl.when(jnp.logical_and(i >= LAG, i < LAG + 8))
         def _():
             j = order(i - LAG)
-            multiply(j, 1 - kind)
-
-            @pl.when(home)
-            def _():
-                to_sibling(j).start()
-
-        k = i - jnp.where(home, LEAD + 1, LAG + 1)
+            for part in range(PARTS):
+                arrival(j, 1 - mine, part).wait_recv()
+            p[j] = product(
+                a_high[...].reshape(768, 768), a_low[...].reshape(768, 768), m[j].reshape(768, 128)
+            ).reshape(2, 384, 128)
+            to_sibling(j).start()
+
+        k = i - (LAG + 1)
 
         @pl.when(jnp.logical_and(k >= 0, k < 8))
         def _():

time: 138 us -> 135 us (0.978)
  the two profiles are of different devices: /device:TPU:2 before, /device:TPU:1 now
where the time goes in v4:
time: 135 us; the launch traced here: 134 us
  Pallas kernels  130 us (96%)
  local copies, waits for them, and re-layouts  3.09 us (2%)
    pallas_call x1, Pallas kernels, on_device(): pl.pallas_call(kernel, out_shape=(jax.ShapeDtypeStruct((384, 128), f32),...  130 us
    unnamed x2, local copies, waits for them, and re-layouts  3.09 us

profile of v4, /device:TPU:1, one launch (start us, length us, event | category | flops | bytes accessed | tf_op | source)
XLA Modules:
  0.0 133.7 jit_solution(8255347460809206540)
XLA Ops:
  0.6 129.9 %shard_map.59 = (f32[384,128]{1,0:T(8,128)}, f32[1,128,128]{2,1,0:T(8,128)}) custom-call(f32[384,768]{1,0:T(8,128)} %a_hbm.1, f32[384,128]{1,0:T(8,128)} %l_hbm.1, s32[1,3]{1,0:T(1,128)} %mask_ref.1, f32[1,128,128]{2,1,0:T(8,128)} %dinv_hbm.1), custom_call_target="tpu_custom_call" | custom-call | flops 3623878656 | bytes 4000000 | tf_op jit(solution)/shard_map/pallas_call | solution.py:399
  130.6 1.6 %copy.8 = f32[384,128]{1,0:T(8,128)} copy(f32[384,128]{1,0:T(8,128)} %get-tuple-element.4) | data formatting | bytes 393216
  132.2 1.5 %copy.9 = f32[1,128,128]{2,1,0:T(8,128)} copy(f32[1,128,128]{2,1,0:T(8,128)} %get-tuple-element.5) | data formatting | bytes 131072

commit v5 on v4

--- a/solution.py
+++ b/solution.py
@@ -10,6 +10,7 @@
 PIECES = 3
 PARTS = 3
 LAG = 3
+ENDS = 3
 PASS = 2
 TRAIL = 4
 
@@ -38,8 +39,8 @@
 
 def kernel(
     a_hbm, l_hbm, mask_ref, dinv_hbm, off_ref, diag_ref,
-    a_ref, l_ref, dinv_ref, masked, turned, a_in, a_high, a_low, m, p, c, far, yr, t, zb, cs, cx, cz, dg,
-    fetch, s_a, r_a, s_first, s_right, s_left, s_x, r_m, s_c, r_c, s_y, r_y, r_far, s_z, r_z,
+    a_ref, l_ref, dinv_ref, masked, turned, a_in, a_high, a_low, m, p, c, far, yr, t, rel, zb, cs, cx, cz, dg,
+    fetch, s_a, r_a, s_first, s_right, s_left, s_x, r_m, s_c, r_c, s_y, r_y, r_far, s_rel, r_rel, s_on, s_z, r_z,
     s_cx, r_cx, s_cz, r_cz, s_dg, r_dg,
 ):
     row, col = lax.axis_index("prow"), lax.axis_index("pcol")
@@ -79,8 +80,20 @@
     def y_peer(step):
         return device(x, zl, zh, lax.rem(y + step, Y), co)
 
-    def end_peer(half):
-        return device(jnp.where(home, x, x_a), zl, half, y, kind)
+    z = zh * ZL + zl
+    way = jnp.where(home, 1, 15)
+    x_end = jnp.where(home, x, x_a)
+
+    def at_z(x, z, co):
+        z = lax.rem(z, 16)
+        return device(x, lax.rem(z, ZL), lax.div(z, ZL), y, co)
+
+    relay = at_z(x, z + way, co)
+    relayed = at_z(x, z + 16 - way, co)
+    relayed_half = lax.div(lax.rem(z + 16 - way, 16), ZL)
+    relay_end = at_z(x_end, z + 16 - way + 8, kind)
+    relay_in = at_z(x_end, z + 8 + way, kind)
+    direct = at_z(x_a, z, 1 - co)
 
     fetch_l = pltpu.make_async_copy(l_hbm, l_ref, fetch.at[0])
     fetch_a = pltpu.make_async_copy(a_hbm, a_ref, fetch.at[1])
@@ -102,11 +115,12 @@
         greet(y_peer(step))
     for step in range(1, ZL):
         greet(z_peer(step))
-    greet(end_peer(1 - zh))
+    greet(relayed)
+    greet(relay_in)
 
     @pl.when(jnp.logical_not(home))
     def _():
-        greet(end_peer(zh))
+        greet(direct)
 
     fetch_l.wait()
     for block in range(3):
@@ -114,7 +128,7 @@
         member = mask_ref[0, block].astype(jnp.float32)
         masked[rows, :] = l_ref[rows, :] * member
 
-    pl.semaphore_wait(barrier, jnp.where(home, 16, 17))
+    pl.semaphore_wait(barrier, jnp.where(home, 17, 18))
 
     def spot(j, half, part):
         return m.at[j, half, pl.ds(part * (384 // PARTS), 384 // PARTS), :]
@@ -195,8 +209,24 @@
             device(x, zl, zh, lax.rem(y - toward + Y, Y), co),
         )
 
-    def to_end(half):
-        return copy_to(t.at[half], zb.at[zh], s_z.at[half], r_z.at[zh], end_peer(half))
+    def third(ref, index, part):
+        return ref.at[index, pl.ds(part * (384 // ENDS), 384 // ENDS), :]
+
+    def to_relay(part):
+        return copy_to(
+            third(t, 1 - zh, part), third(rel, 0, part), s_rel.at[part], r_rel.at[part], relay
+        )
+
+    def send_on(part):
+        return copy_to(
+            third(rel, 0, part), third(zb, relayed_half, part),
+            s_on.at[part], r_z.at[relayed_half, part], relay_end,
+        )
+
+    def to_direct(part):
+        return copy_to(
+            third(t, zh, part), third(zb, zh, part), s_z.at[part], r_z.at[zh, part], direct
+        )
 
     def goes_right(j):
         return jnp.logical_and(j <= zl, zl < 7)
@@ -280,29 +310,45 @@
                         t.at[0], yr.at[half, slot], s_y.at[0], r_y.at[half, slot], sibling
                     ).wait_recv()
                 total = p[j, co] + (yr[half, 0] + yr[half, 1])
-                stays = jnp.logical_and(home, half == zh)
-
-                @pl.when(stays)
+                here = half == zh
+
+                @pl.when(jnp.logical_and(home, here))
                 def _():
                     zb[zh] = total
 
-                @pl.when(jnp.logical_not(stays))
+                @pl.when(jnp.logical_not(jnp.logical_and(home, here)))
                 def _():
                     t[half] = total
-                    to_end(half).start()
+
+                @pl.when(jnp.logical_and(jnp.logical_not(home), here))
+                def _():
+                    for part in range(ENDS):
+                        to_direct(part).start()
+
+                @pl.when(jnp.logical_not(here))
+                def _():
+                    for part in range(ENDS):
+                        to_relay(part).start()
 
         return carry
 
     lax.fori_loop(0, 8 + LAG + 1 + TRAIL, step, 0)
 
-    def end_arrival(half):
-        return copy_to(t.at[0], zb.at[half], s_z.at[0], r_z.at[half], sibling)
-
-    end_arrival(1 - zh).wait_recv()
+    for part in range(ENDS):
+        to_relay(part).wait_recv()
+        send_on(part).start()
+
+    def end_arrival(half, part):
+        here = third(zb, half, part)
+        return copy_to(here, here, s_z.at[0], r_z.at[half, part], sibling)
 
     @pl.when(jnp.logical_not(home))
     def _():
-        end_arrival(zh).wait_recv()
+        for part in range(ENDS):
+            end_arrival(zh, part).wait_recv()
+
+    for part in range(ENDS):
+        end_arrival(1 - zh, part).wait_recv()
 
     for block in range(3):
         rows = pl.ds(block * 128, 128)
@@ -377,11 +423,14 @@
         return carry
 
     lax.fori_loop(0, 8, finish, 0)
-    to_end(1 - zh).wait_send()
+    for part in range(ENDS):
+        to_relay(part).wait_send()
+        send_on(part).wait_send()
 
     @pl.when(jnp.logical_not(home))
     def _():
-        to_end(zh).wait_send()
+        for part in range(ENDS):
+            to_direct(part).wait_send()
 
     for step_ in range(1, X):
         corr_x(step_).wait_send()
@@ -419,6 +468,7 @@
                 pltpu.VMEM((2, 384, 128), f32),
                 pltpu.VMEM((2, 2, 384, 128), f32),
                 pltpu.VMEM((2, 384, 128), f32),
+                pltpu.VMEM((1, 384, 128), f32),
                 pltpu.VMEM((2, 384, 128), f32),
                 pltpu.VMEM((4, 32, 128), f32),
                 pltpu.VMEM((3, 32, 128), f32),
@@ -426,7 +476,8 @@
                 pltpu.VMEM((4, 32, 128), f32),
                 dma((3,)), dma((PIECES,)), dma((PIECES,)), dma((PARTS,)),
                 dma((8, PARTS)), dma((8, PARTS)), dma((8, PARTS)), dma((8, 2, PARTS)),
-                dma((8,)), dma((8,)), dma((8,)), dma((2, 2)), dma((2,)), dma((2,)), dma((2,)),
+                dma((8,)), dma((8,)), dma((8,)), dma((2, 2)), dma((2,)),
+                dma((ENDS,)), dma((ENDS,)), dma((ENDS,)), dma((ENDS,)), dma((2, ENDS)),
                 dma((3,)), dma((3,)), dma((7,)), dma((8,)), dma((3,)), dma((4,)),
             ],
             compiler_params=pltpu.CompilerParams(

time: 135 us -> 143 us (1.059)
  Pallas kernels: 130 us -> 138 us
    pallas_call x1, Pallas kernels: 130 us -> 138 us  [on_device(): pl.pallas_call(kernel, out_shape=(jax.ShapeDtypeStruct((384, 128), f32),...]
where the time goes in v5:
time: 143 us; the launch traced here: 142 us
  Pallas kernels  138 us (97%)
  local copies, waits for them, and re-layouts  3.09 us (2%)
    pallas_call x1, Pallas kernels, on_device(): pl.pallas_call(kernel, out_shape=(jax.ShapeDtypeStruct((384, 128), f32),...  138 us
    unnamed x2, local copies, waits for them, and re-layouts  3.09 us

profile of v5, /device:TPU:1, one launch (start us, length us, event | category | flops | bytes accessed | tf_op | source)
XLA Modules:
  0.0 142.0 jit_solution(9281380229273485012)
XLA Ops:
  0.6 138.2 %shard_map.59 = (f32[384,128]{1,0:T(8,128)}, f32[1,128,128]{2,1,0:T(8,128)}) custom-call(f32[384,768]{1,0:T(8,128)} %a_hbm.1, f32[384,128]{1,0:T(8,128)} %l_hbm.1, s32[1,3]{1,0:T(1,128)} %mask_ref.1, f32[1,128,128]{2,1,0:T(8,128)} %dinv_hbm.1), custom_call_target="tpu_custom_call" | custom-call | flops 3623878656 | bytes 4000000 | tf_op jit(solution)/shard_map/pallas_call | solution.py:448
  138.9 1.6 %copy.8 = f32[384,128]{1,0:T(8,128)} copy(f32[384,128]{1,0:T(8,128)} %get-tuple-element.4) | data formatting | bytes 393216
  140.5 1.5 %copy.9 = f32[1,128,128]{2,1,0:T(8,128)} copy(f32[1,128,128]{2,1,0:T(8,128)} %get-tuple-element.5) | data formatting | bytes 131072

commit v6 on v4

--- a/solution.py
+++ b/solution.py
@@ -8,8 +8,8 @@
 MESH = pl.DeviceIdType.MESH
 X, ZL, ZH, Y = 4, 8, 2, 4
 PIECES = 3
-PARTS = 3
-LAG = 3
+PARTS = 4
+LAG = 2
 PASS = 2
 TRAIL = 4
 
@@ -294,6 +294,38 @@
         return carry
 
     lax.fori_loop(0, 8 + LAG + 1 + TRAIL, step, 0)
+
+    for part in range(PARTS):
+        first(part).wait_send()
+    for piece in range(PIECES):
+        send_a(piece).wait_send()
+
+    def finish(j, carry):
+        to_sibling(j).wait_send()
+        for part in range(PARTS):
+            to_partner(j, part).wait_send()
+
+            @pl.when(goes_right(j))
+            def _(part=part):
+                to_right(j, part).wait_send()
+
+            @pl.when(goes_left(j))
+            def _(part=part):
+                to_left(j, part).wait_send()
+
+        distance, _, _ = role(j)
+
+        @pl.when(distance == 2)
+        def _():
+            to_between(j).wait_send()
+
+        @pl.when(lax.rem(distance, 2) == 1)
+        def _():
+            to_owner(j).wait_send()
+
+        return carry
+
+    lax.fori_loop(0, 8, finish, 0)
 
     def end_arrival(half):
         return copy_to(t.at[0], zb.at[half], s_z.at[0], r_z.at[half], sibling)
@@ -346,37 +378,6 @@
         rows = pl.ds(other * 32, 32)
         diag_ref[0, rows, :] = dinv_ref[0, rows, :] - dg[other]
 
-    for part in range(PARTS):
-        first(part).wait_send()
-    for piece in range(PIECES):
-        send_a(piece).wait_send()
-
-    def finish(j, carry):
-        to_sibling(j).wait_send()
-        for part in range(PARTS):
-            to_partner(j, part).wait_send()
-
-            @pl.when(goes_right(j))
-            def _(part=part):
-                to_right(j, part).wait_send()
-
-            @pl.when(goes_left(j))
-            def _(part=part):
-                to_left(j, part).wait_send()
-
-        distance, _, _ = role(j)
-
-        @pl.when(distance == 2)
-        def _():
-            to_between(j).wait_send()
-
-        @pl.when(lax.rem(distance, 2) == 1)
-        def _():
-            to_owner(j).wait_send()
-
-        return carry
-
-    lax.fori_loop(0, 8, finish, 0)
     to_end(1 - zh).wait_send()
 
     @pl.when(jnp.logical_not(home))

time: 135 us -> 139 us (1.030)
  Pallas kernels: 130 us -> 135 us
    pallas_call x1, Pallas kernels: 130 us -> 135 us  [on_device(): pl.pallas_call(kernel, out_shape=(jax.ShapeDtypeStruct((384, 128), f32),...]
where the time goes in v6:
time: 139 us; the launch traced here: 138 us
  Pallas kernels  135 us (97%)
  local copies, waits for them, and re-layouts  3.09 us (2%)
    pallas_call x1, Pallas kernels, on_device(): pl.pallas_call(kernel, out_shape=(jax.ShapeDtypeStruct((384, 128), f32),...  135 us
    unnamed x2, local copies, waits for them, and re-layouts  3.09 us

profile of v6, /device:TPU:1, one launch (start us, length us, event | category | flops | bytes accessed | tf_op | source)
XLA Modules:
  0.0 138.5 jit_solution(3445355254366808413)
XLA Ops:
  0.6 134.7 %shard_map.59 = (f32[384,128]{1,0:T(8,128)}, f32[1,128,128]{2,1,0:T(8,128)}) custom-call(f32[384,768]{1,0:T(8,128)} %a_hbm.1, f32[384,128]{1,0:T(8,128)} %l_hbm.1, s32[1,3]{1,0:T(1,128)} %mask_ref.1, f32[1,128,128]{2,1,0:T(8,128)} %dinv_hbm.1), custom_call_target="tpu_custom_call" | custom-call | flops 3623878656 | bytes 4000000 | tf_op jit(solution)/shard_map/pallas_call | solution.py:400
  135.4 1.6 %copy.8 = f32[384,128]{1,0:T(8,128)} copy(f32[384,128]{1,0:T(8,128)} %get-tuple-element.4) | data formatting | bytes 393216
  137.0 1.5 %copy.9 = f32[1,128,128]{2,1,0:T(8,128)} copy(f32[1,128,128]{2,1,0:T(8,128)} %get-tuple-element.5) | data formatting | bytes 131072

commit v7 on v6

--- a/solution.py
+++ b/solution.py
@@ -8,8 +8,8 @@
 MESH = pl.DeviceIdType.MESH
 X, ZL, ZH, Y = 4, 8, 2, 4
 PIECES = 3
-PARTS = 4
-LAG = 2
+PARTS = 2
+LAG = 3
 PASS = 2
 TRAIL = 4
 

time: 139 us -> 136 us (0.978)
  Pallas kernels: 135 us -> 131 us
    pallas_call x1, Pallas kernels: 135 us -> 131 us  [on_device(): pl.pallas_call(kernel, out_shape=(jax.ShapeDtypeStruct((384, 128), f32),...]
where the time goes in v7:
time: 136 us; the launch traced here: 135 us
  Pallas kernels  131 us (96%)
  local copies, waits for them, and re-layouts  3.09 us (2%)
    pallas_call x1, Pallas kernels, on_device(): pl.pallas_call(kernel, out_shape=(jax.ShapeDtypeStruct((384, 128), f32),...  131 us
    unnamed x2, local copies, waits for them, and re-layouts  3.09 us

profile of v7, /device:TPU:1, one launch (start us, length us, event | category | flops | bytes accessed | tf_op | source)
XLA Modules:
  0.0 134.7 jit_solution(814548484086356923)
XLA Ops:
  0.6 131.0 %shard_map.59 = (f32[384,128]{1,0:T(8,128)}, f32[1,128,128]{2,1,0:T(8,128)}) custom-call(f32[384,768]{1,0:T(8,128)} %a_hbm.1, f32[384,128]{1,0:T(8,128)} %l_hbm.1, s32[1,3]{1,0:T(1,128)} %mask_ref.1, f32[1,128,128]{2,1,0:T(8,128)} %dinv_hbm.1), custom_call_target="tpu_custom_call" | custom-call | flops 3623878656 | bytes 4000000 | tf_op jit(solution)/shard_map/pallas_call | solution.py:400
  131.7 1.6 %copy.8 = f32[384,128]{1,0:T(8,128)} copy(f32[384,128]{1,0:T(8,128)} %get-tuple-element.4) | data formatting | bytes 393216
  133.3 1.5 %copy.9 = f32[1,128,128]{2,1,0:T(8,128)} copy(f32[1,128,128]{2,1,0:T(8,128)} %get-tuple-element.5) | data formatting | bytes 131072

commit v8 on v7

--- a/solution.py
+++ b/solution.py
@@ -8,7 +8,7 @@
 MESH = pl.DeviceIdType.MESH
 X, ZL, ZH, Y = 4, 8, 2, 4
 PIECES = 3
-PARTS = 2
+PARTS = 3
 LAG = 3
 PASS = 2
 TRAIL = 4
@@ -205,22 +205,31 @@
         return jnp.logical_and(j >= zl, zl > 0)
 
     def step(i, carry):
-        @pl.when(i < 8)
-        def _():
-            j = order(i)
-            right, left = goes_right(j), goes_left(j)
-            for part in range(PARTS):
+        def forward(part, now):
+            @pl.when(jnp.logical_and(i < 8, now))
+            def _():
+                j = order(i)
                 arrival(j, mine, part).wait_recv()
 
-                @pl.when(right)
-                def _(part=part):
+                @pl.when(goes_right(j))
+                def _():
                     to_right(j, part).start()
 
-                @pl.when(left)
-                def _(part=part):
+                @pl.when(goes_left(j))
+                def _():
                     to_left(j, part).start()
 
                 to_partner(j, part).start()
+
+        works = jnp.logical_and(i >= LAG, i < LAG + 8)
+
+        def multiply(j, q):
+            p[j, q] = product(a_high[q], a_low[q], m[j].reshape(768, 128))
+
+        early = i <= LAG
+        forward(0, True)
+        forward(1, early)
+        forward(2, early)
 
         @pl.when(i == LAG)
         def _():
@@ -229,15 +238,21 @@
             high, low = split(a_in[...])
             a_high[1 - kind], a_low[1 - kind] = high, low
 
-        @pl.when(jnp.logical_and(i >= LAG, i < LAG + 8))
+        @pl.when(works)
         def _():
             j = order(i - LAG)
             for part in range(PARTS):
                 arrival(j, 1 - mine, part).wait_recv()
-            p[j] = product(
-                a_high[...].reshape(768, 768), a_low[...].reshape(768, 768), m[j].reshape(768, 128)
-            ).reshape(2, 384, 128)
+            multiply(j, 1 - co)
             to_sibling(j).start()
+
+        forward(1, i > LAG)
+
+        @pl.when(works)
+        def _():
+            multiply(order(i - LAG), co)
+
+        forward(2, i > LAG)
 
         k = i - (LAG + 1)
 

time: 136 us -> 134 us (0.985)
  Pallas kernels: 131 us -> 129 us
    pallas_call x1, Pallas kernels: 131 us -> 129 us  [on_device(): pl.pallas_call(kernel, out_shape=(jax.ShapeDtypeStruct((384, 128), f32),...]
where the time goes in v8:
time: 134 us; the launch traced here: 133 us
  Pallas kernels  129 us (96%)
  local copies, waits for them, and re-layouts  3.09 us (2%)
    pallas_call x1, Pallas kernels, on_device(): pl.pallas_call(kernel, out_shape=(jax.ShapeDtypeStruct((384, 128), f32),...  129 us
    unnamed x2, local copies, waits for them, and re-layouts  3.09 us

profile of v8, /device:TPU:1, one launch (start us, length us, event | category | flops | bytes accessed | tf_op | source)
XLA Modules:
  0.0 132.6 jit_solution(9161572890326253513)
XLA Ops:
  0.6 128.9 %shard_map.59 = (f32[384,128]{1,0:T(8,128)}, f32[1,128,128]{2,1,0:T(8,128)}) custom-call(f32[384,768]{1,0:T(8,128)} %a_hbm.1, f32[384,128]{1,0:T(8,128)} %l_hbm.1, s32[1,3]{1,0:T(1,128)} %mask_ref.1, f32[1,128,128]{2,1,0:T(8,128)} %dinv_hbm.1), custom_call_target="tpu_custom_call" | custom-call | flops 3623878656 | bytes 4000000 | tf_op jit(solution)/shard_map/pallas_call | solution.py:415
  129.5 1.6 %copy.8 = f32[384,128]{1,0:T(8,128)} copy(f32[384,128]{1,0:T(8,128)} %get-tuple-element.4) | data formatting | bytes 393216
  131.1 1.5 %copy.9 = f32[1,128,128]{2,1,0:T(8,128)} copy(f32[1,128,128]{2,1,0:T(8,128)} %get-tuple-element.5) | data formatting | bytes 131072
